TPU v7x, 128 devices: a whole 4x4x4 slice. The times are simulated.
128 devices in a mesh: mem: 16 (over x, z_lo, core), lev: 8 (over y, z_hi).
Axes of the slice: x: 4, y: 4, z: 4 (z_hi: 2, z_lo: 2; z = z_hi * 2 + z_lo), core: 2. Of those that a mesh axis runs over, the one named last changes fastest.
Arguments:
- control_vec: float32 [256, 64, 8192], P('mem', 'lev'), may hold values from -6 to 6
- ens_perturb: bfloat16 [256, 3, 64, 8192], P(None, None, 'lev', 'mem'), may hold values from -6 to 6
- loc_blocks: bfloat16 [64, 9, 128, 128], replicated, may hold values from -0.1875 to 0.1875
- tile_index: int32 [64, 9], replicated, may hold values from 0 to 63, all different within a row
- obs_weight: bfloat16 [3, 64, 256], P(None, 'lev'), may hold values from -0.4375 to 0.4375
- channel_level_mask: int32 [64, 256], P('lev'), may hold values 0 or 1
- obs_precision: float32 [256, 8192], P(None, 'mem'), may hold values from 2 to 64
Outputs:
- hess_vec: float32 [256, 64, 8192], P('mem', 'lev')
Inputs may be any that keep to these rules, and one draw needn't show every extreme that they name: `tile_index`: each row names 9 different tiles; every tile is named by some row.
All inputs are finite; a program needn't handle non-finite values. No bound on the sum of `channel_level_mask` on one device may be relied on, other than what follows from the above.
Results may differ from a plain program's by a relative error of at most 0.012.
Values may be sent and summed in bfloat16 or wider, within the bound.
A program may use at most 192 MiB of HBM per device.

v0:
```python
import math

import jax
import jax.numpy as jnp
from jax import lax
from jax.sharding import PartitionSpec as P


def observe_adjoint(analysis_increment, operator, obs_precision):
    channels = operator.shape[2]
    share = channels // lax.axis_size("lev")
    operator_partial = operator
    local_similarity = lax.psum_scatter(
        jnp.einsum(
            "bws,bwn->sn", operator_partial, analysis_increment, preferred_element_type=jnp.float32
        ),
        "lev",
        scatter_dimension=0,
        tiled=True,
    )
    precision_rows = lax.dynamic_slice_in_dim(
        obs_precision, lax.axis_index("lev") * share, share, 0
    )
    weighted = (precision_rows * local_similarity).astype(jnp.bfloat16)
    operator_partial = operator
    gradient = jnp.einsum(
        "nhs,sb->nhb",
        operator_partial,
        lax.all_gather(weighted, "lev", axis=0, tiled=True),
        preferred_element_type=jnp.float32,
    )
    return gradient.astype(jnp.bfloat16)


def body(
    control_vec, ens_perturb, loc_blocks, tile_index, obs_weight, channel_level_mask, obs_precision
):
    mem_rows, lev_rows, points = control_vec.shape
    tile_len = loc_blocks.shape[2]
    tile_count = points // tile_len
    neighbours = tile_index.shape[1]
    row_total = mem_rows * lev_rows
    control_low = control_vec.astype(jnp.bfloat16).reshape(row_total, tile_count, tile_len)
    blocks = jnp.take(control_low, tile_index, axis=1)
    localized = jnp.einsum("rtkj,tkji->rti", blocks, loc_blocks, preferred_element_type=jnp.float32)
    localized = localized.astype(jnp.bfloat16).reshape(mem_rows, lev_rows, points)
    members = ens_perturb.shape[0]
    ens_scale = 1.0 / math.sqrt(members - 1)
    operator = obs_weight * channel_level_mask.astype(jnp.bfloat16)
    local_pts = lax.all_to_all(localized, "mem", split_axis=2, concat_axis=0, tiled=True)
    analysis_increment = jnp.einsum(
        "mvlp,mlp->vlp", ens_perturb, local_pts, preferred_element_type=jnp.float32
    )
    analysis_increment = (analysis_increment * ens_scale).astype(jnp.bfloat16)
    gradient = observe_adjoint(analysis_increment, operator, obs_precision)
    back_pts = jnp.einsum(
        "mvlp,vlp->mlp", ens_perturb, gradient, preferred_element_type=jnp.float32
    )
    back_pts = (back_pts * ens_scale).astype(jnp.bfloat16)
    backward_values = lax.all_to_all(back_pts, "mem", split_axis=0, concat_axis=2, tiled=True)
    back_tiles = backward_values.reshape(row_total, tile_count, tile_len)
    contrib = jnp.einsum(
        "rti,tkji->rtkj", back_tiles, loc_blocks, preferred_element_type=jnp.float32
    )
    contrib = contrib.reshape(row_total, tile_count * neighbours, tile_len)
    targets = tile_index.reshape(-1)
    adjoint = jnp.zeros((row_total, tile_count, tile_len), jnp.float32).at[:, targets].add(contrib)
    return control_vec + adjoint.reshape(mem_rows, lev_rows, points)


def solution(mesh):
    return jax.shard_map(
        body,
        mesh=mesh,
        in_specs=(
            P("mem", "lev", None),
            P(None, None, "lev", "mem"),
            P(),
            P(),
            P(None, "lev", None),
            P("lev", None),
            P(None, "mem"),
        ),
        out_specs=P("mem", "lev", None),
        check_vma=False,
    )
```

profile of v0, /device:TPU:0, one launch (start us, length us, event | category | flops | bytes accessed | tf_op | source)
XLA Modules:
  0.0 472.0 jit_solution(2274181088321798920)
XLA Ops:
  6.5 0.7 compare_and_fusion
  7.2 0.7 compare_select_fusion
  7.9 0.1 copy.48
  8.1 0.1 copy.49
  8.1 0.1 reshape.61
  8.3 2.6 convert_bitcast_fusion
  10.9 0.6 copy.81
  11.5 1.4 copy.50
  12.8 15.9 %gather_fusion = bf16[576,128,128]{2,1,0:T(8,128)(2,1)} fusion(bf16[128,64,128]{2,0,1:T(8,128)(2,1)S(1)} %copy.50, s32[1024]{0:T(1024)S(1)} %pad_clamp_fusion), kind=kCustom, calls=%fused_computation | custom fusion | bytes 37751040 | tf_op jit(solution)/shard_map/jit(_take)/gather | solution.py:44
  28.8 14.5 %fusion.10 = bf16[128,64,128]{2,0,1:T(8,128)(2,1)S(1)} fusion(bf16[64,9,128,128]{3,2,1,0:T(8,128)(2,1)} %param.9, bf16[64,9,128,128]{3,2,1,0:T(8,128)(2,1)} %bitcast.64, pred[64,9]{1,0:T(8,128)(4,1)S(1)} %copy.48), kind=kOutput, calls=%fused_computation.16 | convolution fusion | flops 2426404864 | bytes 39846464 | tf_op jit(solution)/shard_map/rtkj,tkji->rti/dot_general | solution.py:45
  43.3 2.7 copy.51
  46.0 2.8 reshape.55
  48.8 13.3 %copy.52 = bf16[16,8,8192]{0,1,2:T(8,128)(2,1)} copy(bf16[16,8,8192]{2,1,0:T(8,128)(2,1)S(1)} %reshape.55) | data formatting | bytes 4194304 | tf_op jit(solution)/shard_map/reshape | solution.py:46
  62.1 20.8 %reshape.86 = bf16[16,2,32768]{2,1,0:T(2,128)(2,1)} reshape(bf16[8192,8,16]{2,1,0:T(8,128)(2,1)} %bitcast.62) | data formatting | bytes 4194304
  82.9 0.0 copy-start.2
  82.9 6.0 %all-to-all-start = ((bf16[16,2,32768]{2,1,0:T(2,128)(2,1)}), bf16[16,2,32768]{2,1,0:T(2,128)(2,1)S(1)}, u32[]{:S(2)}, u32[]{:S(2)}) async-start(bf16[16,2,32768]{2,1,0:T(2,128)(2,1)} %reshape.86), calls=%async_computation | async-start | bytes 4194304 | tf_op jit(solution)/shard_map/all_to_all | solution.py:50
  88.9 0.2 reduce-scatter.2.cloned.1.call-start
  89.1 0.0 copy-done.2
  89.1 27.5 %all-to-all-done = bf16[16,2,32768]{2,1,0:T(2,128)(2,1)S(1)} async-done(((bf16[16,2,32768]{2,1,0:T(2,128)(2,1)}), bf16[16,2,32768]{2,1,0:T(2,128)(2,1)S(1)}, u32[]{:S(2)}, u32[]{:S(2)}) %all-to-all-start) | async-done | bytes 2097184 | tf_op jit(solution)/shard_map/all_to_all | solution.py:50
  116.6 14.4 %reshape.87 = bf16[8192,8,16]{2,1,0:T(8,128)(2,1)} reshape(bf16[16,2,32768]{2,1,0:T(2,128)(2,1)S(1)} %all-to-all-done) | data formatting | bytes 4194304
  131.0 17.5 %copy.76 = bf16[16,16,8,512]{3,2,1,0:T(8,128)(2,1)S(1)} copy(bf16[16,16,8,512]{1,2,3,0:T(8,128)(2,1)} %bitcast.63) | data formatting | bytes 4194304
  148.5 0.7 bitcast_convert_fusion.1
  149.2 0.0 copy-start.1
  149.2 4.4 multiply_reduce_fusion.1
  153.6 0.0 copy-done.1
  153.6 1.1 convolution_bitcast_fusion
  154.7 0.0 reduce-scatter.2.cloned.1.call-update
  154.7 72.5 %reduce-scatter.2.cloned.1.call-done = f32[32,512]{1,0:T(8,128)} async-done(((f32[256,512]{1,0:T(8,128)}), f32[32,512]{1,0:T(8,128)}) %reduce-scatter.2.cloned.1.call-update) | async-done | bytes 65552 | tf_op jit(solution)/shard_map/reduce_scatter | solution.py:13
  227.2 0.9 multiply_convert_fusion.1
  228.1 34.4 %all_gather.3 = bf16[256,512]{1,0:T(8,128)(2,1)S(1)} all-gather(bf16[32,512]{1,0:T(8,128)(2,1)S(1)} %multiply_convert_fusion.1), channel_id=1, replica_groups=mesh['mem'=16,'lev'=8] {'lev'}, dimensions={0}, use_global_device_ids=true | all-gather | bytes 294912 | tf_op jit(solution)/shard_map/all_gather | solution.py:29
  262.5 0.1 fusion.14
  262.7 5.5 %multiply_reduce_fusion = f32[8,512,256]{1,0,2:T(8,128)S(1)} fusion(f32[8,512,3]{1,0,2:T(8,128)S(1)} %fusion.14, bf16[256,3,8,512]{3,2,1,0:T(8,128)(2,1)} %param.8), kind=kLoop, calls=%fused_computation.6 | loop fusion | flops 8388608 | bytes 10534912 | tf_op jit(solution)/shard_map/mvlp,vlp->mlp/dot_general | solution.py:56
  268.1 0.0 copy-start
  268.2 2.0 fusion.7
  270.1 4.6 all-to-all-start.1
  274.8 0.0 copy-done
  274.8 0.1 copy.47
  274.9 0.1 reshape.53
  275.0 27.5 %all-to-all-done.1 = bf16[256,8,512]{2,1,0:T(8,128)(2,1)S(1)} async-done(((bf16[256,8,512]{2,1,0:T(8,128)(2,1)}), bf16[256,8,512]{2,1,0:T(8,128)(2,1)S(1)}, u32[]{:S(2)}, u32[]{:S(2)}) %all-to-all-start.1) | async-done | bytes 2097184 | tf_op jit(solution)/shard_map/all_to_all | solution.py:60
  302.5 2.5 copy.55
  305.0 3.1 reshape.56
  308.1 20.8 %fusion.8 = f32[64,128,9,128]{3,1,2,0:T(8,128)} fusion(bf16[64,9,128,128]{3,2,1,0:T(8,128)(2,1)} %param.9, bf16[128,64,128,1]{2,1,0,3:T(8,128)(2,1)S(1)} %bitcast.65), kind=kOutput, calls=%fused_computation.12 | convolution fusion | flops 2415919104 | bytes 58720256 | tf_op jit(solution)/shard_map/rti,tkji->rtkj/dot_general | solution.py:62
  328.9 2.5 broadcast_in_dim.17
  331.4 116.3 %scatter_fusion = f32[128,64,128]{2,0,1:T(8,128)} fusion(f32[128,64,128]{2,0,1:T(8,128)} %broadcast_in_dim.17, s32[576]{0:T(1024)S(1)} %fusion.23, f32[576,128,128]{2,1,0:T(8,128)} %bitcast.61), kind=kCustom, calls=%fused_computation.1 | custom fusion | flops 9437184 | bytes 113248512 | tf_op jit(solution)/shard_map/scatter-add | solution.py:67
  447.7 6.5 %copy.57 = f32[128,64,128]{2,1,0:T(8,128)} copy(f32[128,64,128]{2,0,1:T(8,128)} %scatter_fusion) | data formatting | bytes 8388608 | tf_op jit(solution)/shard_map/scatter-add | solution.py:67
  454.3 4.9 %reshape.58 = f32[16,8,8192]{2,1,0:T(8,128)} reshape(f32[128,64,128]{2,1,0:T(8,128)} %copy.57) | data formatting | bytes 8388608 | tf_op jit(solution)/shard_map/reshape | solution.py:68
  459.2 6.0 %add.36 = f32[16,8,8192]{2,1,0:T(8,128)} add(f32[16,8,8192]{2,1,0:T(8,128)} %param.7, f32[16,8,8192]{2,1,0:T(8,128)} %reshape.58) | non-fusion elementwise | flops 1048576 | bytes 12582912 | tf_op jit(solution)/shard_map/add | solution.py:68
  (3 shorter events, 0.0 us)
Async XLA Ops:
  82.9 6.2 %copy-start.2 = (s32[8,256]{1,0:T(8,128)S(1)}, s32[8,256]{1,0:T(8,128)}, u32[]{:S(2)}) copy-start(s32[8,256]{1,0:T(8,128)} %param.12) | copy-start | bytes 24580
  82.9 33.7 %all-to-all-start = ((bf16[16,2,32768]{2,1,0:T(2,128)(2,1)}), bf16[16,2,32768]{2,1,0:T(2,128)(2,1)S(1)}, u32[]{:S(2)}, u32[]{:S(2)}) async-start(bf16[16,2,32768]{2,1,0:T(2,128)(2,1)} %reshape.86), calls=%async_computation | async-start | bytes 4194304 | tf_op jit(solution)/shard_map/all_to_all | solution.py:50
  88.9 138.4 %reduce-scatter.2.cloned.1.call-start = ((), (), s32[]{:S(2)}) async-start(), calls=%async_computation.3 | async-start | bytes 589824 | tf_op jit(solution)/shard_map/reduce_scatter | solution.py:13
  149.2 4.4 copy-start.1
  268.1 6.6 %copy-start = (s32[64,9]{0,1:T(8,128)S(1)}, s32[64,9]{0,1:T(8,128)}, u32[]{:S(2)}) copy-start(s32[64,9]{0,1:T(8,128)} %param.10) | copy-start | bytes 6916
  270.1 32.4 %all-to-all-start.1 = ((bf16[256,8,512]{2,1,0:T(8,128)(2,1)}), bf16[256,8,512]{2,1,0:T(8,128)(2,1)S(1)}, u32[]{:S(2)}, u32[]{:S(2)}) async-start(bf16[256,8,512]{2,1,0:T(8,128)(2,1)} %fusion.7), calls=%async_computation.2 | async-start | bytes 4194304 | tf_op jit(solution)/shard_map/all_to_all | solution.py:60
Sparse Core Ops, SparseCore 0:
  154.8 72.3 reduce-scatter.1
where the time goes:
time: 476 us; the launch traced here: 472 us
  other arithmetic  140 us (29%)
  waiting for transfers between devices  128 us (27%)
  local copies, waits for them, and re-layouts  109 us (23%)
  matrix products  36.5 us (8%)
  blocking collectives  34.4 us (7%)
  between operations  13.6 us (3%)
  starting transfers between devices  10.8 us (2%)
    scatter-add x1, other arithmetic, body(): jnp.zeros((row_total, tile_count, tile_len), jnp.float32).at[:, targets]  116 us
    reduce_scatter x1, waiting for transfers between devices, observe_adjoint(): lax.psum_scatter(jnp.einsum('bws,bwn->sn', operator_partial, analysis_inc...  72.5 us
    unnamed x11, local copies, waits for them, and re-layouts  53.3 us
    all_gather x1, blocking collectives, observe_adjoint(): lax.all_gather(weighted, 'lev', axis=0, tiled=True)  34.4 us
    all_to_all x1, waiting for transfers between devices, body(): lax.all_to_all(localized, 'mem', split_axis=2, concat_axis=0, tiled=True)  27.5 us
    all_to_all x1, waiting for transfers between devices, body(): lax.all_to_all(back_pts, 'mem', split_axis=0, concat_axis=2, tiled=True)  27.5 us
    dot_general x1, matrix products, body(): jnp.einsum('rti,tkji->rtkj', back_tiles, loc_blocks, preferred_element_ty...  20.8 us
    reshape x2, local copies, waits for them, and re-layouts, body(): localized.astype(jnp.bfloat16).reshape(mem_rows, lev_rows, points)  16.1 us
  transfers between devices with their start and end apart: 3, of which 3 were waited for; matrix products, arithmetic and copies ran while one was open for 0% of the time, Pallas kernels for 0%

commit v1 on v0

v1 whole, which is shorter than its diff:
```python
import functools
import math

import jax
import jax.numpy as jnp
from jax import lax
from jax.experimental import pallas as pl
from jax.experimental.pallas import tpu as pltpu
from jax.sharding import PartitionSpec as P

MESH = pl.DeviceIdType.MESH
TILE = 128
PAD = 32


def exchange_kernel(
    geo, idx_ref, ctrl_hbm, ens_hbm, loc_hbm, obs_ref, mask_ref, prec_ref, back_hbm,
    ctrl32, ctrl, loc, ens, send, recv, bsend, opg, incg,
    ctrl_sem, loc_sem, ens_sem, own_sem, fsend, frecv, bsend_sem, brecv_sem, osend, orecv, isend, irecv,
):
    n_mem, n_lev, chunks, neigh, scale = geo
    me = lax.axis_index("mem")
    lev = lax.axis_index("lev")
    rows = ctrl32.shape[0]
    tiles = ctrl.shape[0]
    members = n_mem * (rows // 8)
    per_dev = rows * 3
    groups = ctrl_sem.shape[0]
    span = ctrl32.shape[1] // groups

    def peer(i, sign):
        dx, dz, dc = 3 - i % 4, 1 - i // 8, 1 - (i // 4) % 2
        x, z, c = me // 4, (me // 2) % 2, me % 2
        return ((x + sign * dx + 4) % 4) * 4 + ((z + dz) % 2) * 2 + (c + dc) % 2

    barrier = pltpu.get_barrier_semaphore()
    for i in range(n_mem - 1):
        pl.semaphore_signal(barrier, inc=1, device_id={"mem": peer(i, 1)}, device_id_type=MESH)
    for j in range(1, n_lev):
        pl.semaphore_signal(barrier, inc=1, device_id={"lev": (lev + j) % n_lev}, device_id_type=MESH)

    def ctrl_copy(g):
        cols = pl.ds(pl.multiple_of(g * span, TILE), span)
        return pltpu.make_async_copy(ctrl_hbm.at[:, cols], ctrl32.at[:, cols], ctrl_sem.at[g])

    def loc_copy(n):
        t = peer(n % n_mem, 1) * chunks + n // n_mem
        return pltpu.make_async_copy(loc_hbm.at[t], loc.at[t], loc_sem.at[n])

    def start(fn):
        def go(n, carry):
            fn(n).start()
            return carry
        return go

    lax.fori_loop(0, groups, start(ctrl_copy), 0)
    lax.fori_loop(0, tiles, start(loc_copy), 0)
    ens_copy = pltpu.make_async_copy(ens_hbm, ens, ens_sem)
    ens_copy.start()

    op = obs_ref[...].astype(jnp.float32) * mask_ref[...].astype(jnp.float32)[None]
    op = op.reshape(24, op.shape[2])
    op = jnp.concatenate([op, jnp.zeros((PAD - 24, op.shape[1]), jnp.float32)], axis=0)
    mine = pl.ds(pl.multiple_of(lev * PAD, PAD), PAD)
    opg[mine, :] = op.astype(jnp.bfloat16)

    per_group = span // TILE

    def convert(g, carry):
        ctrl_copy(g).wait()
        for u in range(per_group):
            s = g * per_group + u
            cols = pl.ds(pl.multiple_of(s * TILE, TILE), TILE)
            ctrl[s] = ctrl32[:, cols].astype(jnp.bfloat16)
        return carry

    lax.fori_loop(0, groups, convert, 0)
    pl.semaphore_wait(barrier, n_mem - 1 + n_lev - 1)

    def op_copy(j):
        return pltpu.make_async_remote_copy(
            src_ref=opg.at[mine], dst_ref=opg.at[mine], send_sem=osend.at[j], recv_sem=orecv.at[j],
            device_id={"lev": (lev + j) % n_lev}, device_id_type=MESH,
        )

    def inc_copy(c, j):
        return pltpu.make_async_remote_copy(
            src_ref=incg.at[c, mine], dst_ref=incg.at[c, mine],
            send_sem=isend.at[c, j], recv_sem=irecv.at[c, j],
            device_id={"lev": (lev + j) % n_lev}, device_id_type=MESH,
        )

    def fwd_copy(c, i):
        d = peer(i, 1)
        return pltpu.make_async_remote_copy(
            src_ref=send.at[c, d], dst_ref=recv.at[c, me], send_sem=fsend.at[c, i], recv_sem=frecv.at[c, i],
            device_id={"mem": d}, device_id_type=MESH,
        )

    def bwd_copy(c, i):
        d = peer(i, 1)
        return pltpu.make_async_remote_copy(
            src_ref=bsend.at[c, d], dst_ref=back_hbm.at[c, me], send_sem=bsend_sem.at[c, i],
            recv_sem=brecv_sem.at[c, i], device_id={"mem": d}, device_id_type=MESH,
        )

    for j in range(1, n_lev):
        op_copy(j).start()

    def localize(c, i):
        t = peer(i, 1) * chunks + c
        loc_copy(c * n_mem + i).wait()
        picked = jnp.concatenate([ctrl[idx_ref[t, k]] for k in range(neigh)], axis=1)
        out = jnp.dot(picked, loc[t], preferred_element_type=jnp.float32)
        return out.astype(jnp.bfloat16)

    def fwd(c):
        def step(i, carry):
            send[c, peer(i, 1)] = localize(c, i)
            fwd_copy(c, i).start()
            return carry

        lax.fori_loop(0, n_mem - 1, step, 0)
        recv[c, me] = localize(c, n_mem - 1)

    def part(c, src, acc):
        cols = pl.ds(c * TILE, TILE)
        weights = recv[c, src].astype(jnp.float32).reshape(rows // 8, 1, 8, TILE)
        pert = ens[pl.ds(pl.multiple_of(src * per_dev, per_dev), per_dev), cols]
        pert = pert.astype(jnp.float32).reshape(rows // 8, 3, 8, TILE)
        return acc + jnp.sum(pert * weights, axis=0)

    def increment(c):
        acc = part(c, me, jnp.zeros((3, 8, TILE), jnp.float32))

        def step(i, acc):
            fwd_copy(c, i).wait_recv()
            return part(c, peer(i, -1), acc)

        acc = lax.fori_loop(0, n_mem - 1, step, acc) * scale
        acc = jnp.concatenate([acc.reshape(24, TILE), jnp.zeros((PAD - 24, TILE), jnp.float32)], axis=0)
        incg[c, mine, :] = acc.astype(jnp.bfloat16)
        for j in range(1, n_lev):
            inc_copy(c, j).start()

    def observe(c):
        for j in range(1, n_lev):
            inc_copy(c, j).wait_recv()
        evolved = lax.dot_general(
            opg[...], incg[c], (((0,), (0,)), ((), ())), preferred_element_type=jnp.float32
        )
        weighted = (prec_ref[:, pl.ds(c * TILE, TILE)] * evolved).astype(jnp.bfloat16)
        grad = jnp.dot(opg[mine, :], weighted, preferred_element_type=jnp.float32)
        grad = grad.astype(jnp.bfloat16).astype(jnp.float32)[:24].reshape(1, 3, 8, TILE)

        def back(d):
            cols = pl.ds(c * TILE, TILE)
            pert = ens[pl.ds(pl.multiple_of(d * per_dev, per_dev), per_dev), cols]
            pert = pert.astype(jnp.float32).reshape(rows // 8, 3, 8, TILE)
            out = jnp.sum(pert * grad, axis=1) * scale
            bsend[c, d] = out.reshape(rows, TILE).astype(jnp.bfloat16)

        def step(i, carry):
            back(peer(i, 1))
            bwd_copy(c, i).start()
            return carry

        lax.fori_loop(0, n_mem - 1, step, 0)
        back(me)
        pltpu.make_async_copy(bsend.at[c, me], back_hbm.at[c, me], own_sem.at[c]).start()

    for c in range(chunks):
        fwd(c)
    ens_copy.wait()
    for j in range(1, n_lev):
        op_copy(j).wait()
    for c in range(chunks):
        increment(c)
        observe(c)

    for c in range(chunks):
        pltpu.make_async_copy(bsend.at[c, me], back_hbm.at[c, me], own_sem.at[c]).wait()

        def finish(i, carry):
            fwd_copy(c, i).wait_send()
            bwd_copy(c, i).wait()
            return carry

        lax.fori_loop(0, n_mem - 1, finish, 0)
        for j in range(1, n_lev):
            inc_copy(c, j).wait_send()


def adjoint_kernel(chunks, neigh, idx_ref, ctrl_hbm, back_ref, loc_hbm, out_hbm, acc, loc, ctrl_sem, loc_sem, out_sem):
    tiles = loc.shape[0]
    groups = loc_sem.shape[0]
    per_group = tiles // groups

    def loc_copy(g):
        at = pl.ds(g * per_group, per_group)
        return pltpu.make_async_copy(loc_hbm.at[at], loc.at[at], loc_sem.at[g])

    ctrl_copy = pltpu.make_async_copy(ctrl_hbm, acc, ctrl_sem)
    loc_copy(0).start()
    ctrl_copy.start()
    for g in range(1, groups):
        loc_copy(g).start()
    ctrl_copy.wait()

    def group(g, carry):
        loc_copy(g).wait()
        for u in range(per_group):
            t = g * per_group + u
            vals = lax.dot_general(
                back_ref[t % chunks, t // chunks], loc[t], (((1,), (1,)), ((), ())),
                preferred_element_type=jnp.float32,
            )
            for k in range(neigh):
                cols = pl.ds(pl.multiple_of(idx_ref[t, k] * TILE, TILE), TILE)
                acc[:, cols] += vals[:, k * TILE : (k + 1) * TILE]
        return carry

    lax.fori_loop(0, groups, group, 0)
    out = pltpu.make_async_copy(acc, out_hbm, out_sem)
    out.start()
    out.wait()


def body(n_mem, n_lev, control_vec, ens_perturb, loc_blocks, tile_index, obs_weight, channel_level_mask, obs_precision):
    mem_rows, lev_rows, points = control_vec.shape
    members = ens_perturb.shape[0]
    tiles, neigh = tile_index.shape
    chunks = tiles // n_mem
    rows = mem_rows * lev_rows
    channels = obs_weight.shape[2]
    control = control_vec.reshape(rows, points)
    ens = ens_perturb.reshape(members * 3 * lev_rows, points // n_mem)
    loc = loc_blocks.reshape(tiles, neigh * TILE, TILE)
    hbm = pl.BlockSpec(memory_space=pl.ANY)
    vmem = pl.BlockSpec(memory_space=pltpu.VMEM)
    smem = pl.BlockSpec(memory_space=pltpu.SMEM)
    dma = pltpu.SemaphoreType.DMA
    geo = (n_mem, n_lev, chunks, neigh, 1.0 / math.sqrt(members - 1))
    wide = (chunks, n_mem, rows, TILE)
    back = pl.pallas_call(
        functools.partial(exchange_kernel, geo),
        out_shape=jax.ShapeDtypeStruct(wide, jnp.bfloat16),
        in_specs=[smem, hbm, hbm, hbm, vmem, vmem, vmem],
        out_specs=hbm,
        scratch_shapes=[
            pltpu.VMEM((rows, points), jnp.float32),
            pltpu.VMEM((tiles, rows, TILE), jnp.bfloat16),
            pltpu.VMEM(loc.shape, jnp.bfloat16),
            pltpu.VMEM(ens.shape, jnp.bfloat16),
            pltpu.VMEM(wide, jnp.bfloat16),
            pltpu.VMEM(wide, jnp.bfloat16),
            pltpu.VMEM(wide, jnp.bfloat16),
            pltpu.VMEM((n_lev * PAD, channels), jnp.bfloat16),
            pltpu.VMEM((chunks, n_lev * PAD, TILE), jnp.bfloat16),
            dma((8,)), dma((tiles,)), dma, dma((chunks,)),
            dma((chunks, n_mem)), dma((chunks, n_mem)), dma((chunks, n_mem)), dma((chunks, n_mem)),
            dma((n_lev,)), dma((n_lev,)), dma((chunks, n_lev)), dma((chunks, n_lev)),
        ],
        compiler_params=pltpu.CompilerParams(
            collective_id=0, has_side_effects=True, vmem_limit_bytes=56 * 2**20
        ),
        name="exchange",
    )(tile_index, control, ens, loc, obs_weight, channel_level_mask, obs_precision)
    out = pl.pallas_call(
        functools.partial(adjoint_kernel, chunks, neigh),
        out_shape=jax.ShapeDtypeStruct((rows, points), jnp.float32),
        in_specs=[smem, hbm, vmem, hbm],
        out_specs=hbm,
        scratch_shapes=[
            pltpu.VMEM((rows, points), jnp.float32),
            pltpu.VMEM(loc.shape, jnp.bfloat16),
            dma, dma((16,)), dma,
        ],
        compiler_params=pltpu.CompilerParams(vmem_limit_bytes=48 * 2**20),
        name="adjoint",
    )(tile_index, control, back, loc)
    return out.reshape(control_vec.shape)


def solution(mesh):
    return jax.shard_map(
        functools.partial(body, mesh.shape["mem"], mesh.shape["lev"]),
        mesh=mesh,
        in_specs=(
            P("mem", "lev", None),
            P(None, None, "lev", "mem"),
            P(),
            P(),
            P(None, "lev", None),
            P("lev", None),
            P(None, "mem"),
        ),
        out_specs=P("mem", "lev", None),
        check_vma=False,
    )
```

time: 476 us -> 101 us (0.21)
  other arithmetic: 140 us -> 0 us
  waiting for transfers between devices: 128 us -> 0 us
  local copies, waits for them, and re-layouts: 109 us -> 2.98 us
  Pallas kernels: 0 us -> 97.8 us
  matrix products: 36.5 us -> 0 us
  blocking collectives: 34.4 us -> 0 us
  between operations: 13.6 us -> 0.03 us
  starting transfers between devices: 10.8 us -> 0 us
    scatter-add x1 -> x0, other arithmetic: 116 us -> none  [body(): jnp.zeros((row_total, tile_count, tile_len), jnp.float32).at[:, targets]]
    pallas_call x0 -> x2, Pallas kernels: none -> 97.8 us  [the longest x1 75.5 us: body(): pl.pallas_call(functools.partial(exchange_kernel, geo), out_shape=jax.Sha...]
    reduce_scatter x1 -> x0, waiting for transfers between devices: 72.5 us -> none  [observe_adjoint(): lax.psum_scatter(jnp.einsum('bws,bwn->sn', operator_partial, analysis_inc...]
    all_to_all x2 -> x0, waiting for transfers between devices: 55 us -> none  [the longest x1 27.5 us: body(): lax.all_to_all(localized, 'mem', split_axis=2, concat_axis=0, tiled=True)]
    unnamed x11 -> x5, local copies, waits for them, and re-layouts: 53.3 us -> 2.98 us
    dot_general x4 -> x0, matrix products: 36.5 us -> none  [the longest x1 20.8 us: body(): jnp.einsum('rti,tkji->rtkj', back_tiles, loc_blocks, preferred_element_ty...]
    all_gather x1 -> x0, blocking collectives: 34.4 us -> none  [observe_adjoint(): lax.all_gather(weighted, 'lev', axis=0, tiled=True)]
    reshape x6 -> x0, local copies, waits for them, and re-layouts: 25.7 us -> none  [the longest x2 16.1 us: body(): localized.astype(jnp.bfloat16).reshape(mem_rows, lev_rows, points)]
  transfers between devices with their start and end apart: 3 -> 0, of which waited for: 3 -> 0; matrix products, arithmetic and copies ran while one was open for 0% -> 0% of each run, Pallas kernels for 0% -> 0%
where the time goes in v1:
time: 101 us
  Pallas kernels  97.8 us (97%)
  local copies, waits for them, and re-layouts  2.98 us (3%)
    pallas_call x1, Pallas kernels, body(): pl.pallas_call(functools.partial(exchange_kernel, geo), out_shape=jax.Sha...  75.5 us
    pallas_call x1, Pallas kernels, body(): pl.pallas_call(functools.partial(adjoint_kernel, chunks, neigh), out_shap...  22.3 us
    unnamed x5, local copies, waits for them, and re-layouts  2.98 us

profile of v1, /device:TPU:0, one launch (start us, length us, event | category | flops | bytes accessed | tf_op | source)
XLA Modules:
  0.0 100.8 jit_solution(12059947557315912528)
XLA Ops:
  0.0 1.4 %copy.9.idx_ref = s32[64,9]{1,0:T(8,128)} copy(s32[64,9]{0,1:T(8,128)} %param.10) | data formatting | bytes 4608 | tf_op args[3]
  1.4 0.0 copy-start.1
  1.4 75.5 %exchange.1.back_ref = bf16[4,16,128,128]{3,2,1,0:T(8,128)(2,1)} custom-call(s32[64,9]{1,0:T(8,128)} %copy.9.idx_ref, f32[128,8192]{1,0:T(8,128)} %bitcast.6, bf16[6144,512]{1,0:T(8,128)(2,1)} %bitcast.8, bf16[64,1152,128]{2,1,0:T(8,128)(2,1)} %bitcast.4, bf16[3,8,256]{2,1,0:T(8,128)(2,1)} %obs_ref.1, s32[8,256]{1,0:T(8,128)} %mask_ref.1, f32[256,512]{1,0:T(8,128)} %prec_ref.1), custom_call_target="tpu_custom_call" | custom-call | tf_op jit(solution)/shard_map/exchange/pallas_call | solution.py:245
  76.9 0.0 copy-done.1
  76.9 0.0 copy-start
  77.0 1.6 %copy-done = bf16[4,16,128,128]{3,2,1,0:T(8,128)(2,1)S(1)} copy-done((bf16[4,16,128,128]{3,2,1,0:T(8,128)(2,1)S(1)}, bf16[4,16,128,128]{3,2,1,0:T(8,128)(2,1)}, u32[]{:S(2)}) %copy-start) | copy-done | bytes 2097176
  78.5 22.3 %adjoint.1 = f32[128,8192]{1,0:T(8,128)} custom-call(s32[64,9]{1,0:T(8,128)S(1)} %copy-done.1, f32[128,8192]{1,0:T(8,128)} %bitcast.7, bf16[4,16,128,128]{3,2,1,0:T(8,128)(2,1)S(1)} %copy-done, bf16[64,1152,128]{2,1,0:T(8,128)(2,1)} %bitcast.5), custom_call_target="tpu_custom_call" | custom-call | tf_op jit(solution)/shard_map/adjoint/pallas_call | solution.py:269
Async XLA Ops:
  1.4 75.5 %copy-start.1 = (s32[64,9]{1,0:T(8,128)S(1)}, s32[64,9]{1,0:T(8,128)}, u32[]{:S(2)}) copy-start(s32[64,9]{1,0:T(8,128)} %copy.9.idx_ref) | copy-start | bytes 6916
  76.9 1.6 %copy-start = (bf16[4,16,128,128]{3,2,1,0:T(8,128)(2,1)S(1)}, bf16[4,16,128,128]{3,2,1,0:T(8,128)(2,1)}, u32[]{:S(2)}) copy-start(bf16[4,16,128,128]{3,2,1,0:T(8,128)(2,1)} %exchange.1.back_ref) | copy-start | bytes 6291460

commit v2 on v1

v2 whole, which is shorter than its diff:
```python
import functools
import math

import jax
import jax.numpy as jnp
from jax import lax
from jax.experimental import pallas as pl
from jax.experimental.pallas import tpu as pltpu
from jax.sharding import PartitionSpec as P

MESH = pl.DeviceIdType.MESH
TILE = 128
PAD = 32
AHEAD = 3


def exchange_kernel(
    geo, idx_ref, ctrl_hbm, ens_hbm, loc_hbm, obs_ref, mask_ref, prec_hbm, back_hbm,
    prec_ref, prec_sem, ctrl32, ctrl, loc, ens, send, recv, bsend, opg, incg,
    ctrl_sem, loc_sem, ens_sem, own_sem, fsend, frecv, bsend_sem, brecv_sem, osend, orecv, isend, irecv,
):
    n_mem, n_lev, chunks, neigh, scale = geo
    me = lax.axis_index("mem")
    lev = lax.axis_index("lev")
    my_x, my_z, my_c = lax.div(me, 4), lax.rem(lax.div(me, 2), 2), lax.rem(me, 2)
    rows = ctrl32.shape[0]
    per_dev = rows * 3
    groups = ctrl_sem.shape[0]
    span = ctrl32.shape[1] // groups

    def zc_of(g):
        return lax.rem(my_z + 1 - lax.div(g, 2), 2) * 2 + lax.rem(my_c + 1 - lax.rem(g, 2), 2)

    def peer(i):
        return lax.rem(my_x + 3 - lax.rem(i, 4), 4) * 4 + zc_of(lax.div(i, 4))

    def source(i):
        return lax.rem(my_x + 1 + lax.rem(i, 4), 4) * 4 + zc_of(lax.div(i, 4))

    def level_peer(j):
        return {"lev": lax.rem(lev + j, n_lev)}

    def ctrl_copy(g):
        cols = pl.ds(pl.multiple_of(g * span, TILE), span)
        return pltpu.make_async_copy(ctrl_hbm.at[:, cols], ctrl32.at[:, cols], ctrl_sem.at[g])

    def loc_copy(n):
        c, zc = lax.div(n, 4), zc_of(lax.rem(n, 4))
        return pltpu.make_async_copy(loc_hbm.at[:, zc, c], loc.at[c, zc], loc_sem.at[n])

    def repeat(lo, hi, fn):
        def step(n, carry):
            fn(n)
            return carry

        lax.fori_loop(lo, hi, step, 0)

    repeat(0, groups, lambda g: ctrl_copy(g).start())
    loc_copy(0).start()
    barrier = pltpu.get_barrier_semaphore()
    for i in range(n_mem - 1):
        pl.semaphore_signal(barrier, inc=1, device_id={"mem": peer(i)}, device_id_type=MESH)
    for j in range(1, n_lev):
        pl.semaphore_signal(barrier, inc=1, device_id=level_peer(j), device_id_type=MESH)
    ens_copy = pltpu.make_async_copy(ens_hbm, ens, ens_sem)
    prec_copy = pltpu.make_async_copy(prec_hbm, prec_ref, prec_sem)

    op = obs_ref[...].astype(jnp.float32) * mask_ref[...].astype(jnp.float32)[None]
    op = op.reshape(24, op.shape[2])
    op = jnp.concatenate([op, jnp.zeros((PAD - 24, op.shape[1]), jnp.float32)], axis=0)
    mine = pl.ds(pl.multiple_of(lev * PAD, PAD), PAD)
    opg[mine, :] = op.astype(jnp.bfloat16)

    per_group = span // TILE

    def convert(g):
        ctrl_copy(g).wait()
        loc_copy(g + 1).start()
        for u in range(per_group):
            s = g * per_group + u
            cols = pl.ds(pl.multiple_of(s * TILE, TILE), TILE)
            ctrl[s] = ctrl32[:, cols].astype(jnp.bfloat16)

    repeat(0, groups, convert)

    def op_copy(j):
        return pltpu.make_async_remote_copy(
            src_ref=opg.at[mine], dst_ref=opg.at[mine], send_sem=osend.at[j], recv_sem=orecv.at[j],
            device_id=level_peer(j), device_id_type=MESH,
        )

    def inc_copy(c, j):
        return pltpu.make_async_remote_copy(
            src_ref=incg.at[c, mine], dst_ref=incg.at[c, mine],
            send_sem=isend.at[c, j], recv_sem=irecv.at[c, j],
            device_id=level_peer(j), device_id_type=MESH,
        )

    def fwd_copy(c, i):
        d = peer(i)
        return pltpu.make_async_remote_copy(
            src_ref=send.at[c, d], dst_ref=recv.at[c, me], send_sem=fsend.at[c, i], recv_sem=frecv.at[c, i],
            device_id={"mem": d}, device_id_type=MESH,
        )

    def bwd_copy(c, i):
        d = peer(i)
        return pltpu.make_async_remote_copy(
            src_ref=bsend.at[c, d], dst_ref=back_hbm.at[c, me], send_sem=bsend_sem.at[c, i],
            recv_sem=brecv_sem.at[c, i], device_id={"mem": d}, device_id_type=MESH,
        )

    def localize(n):
        c, zc = lax.div(n, 4), zc_of(lax.rem(n, 4))
        loc_copy(n).wait()
        for u in range(4):
            x = lax.rem(my_x + 3 - u, 4)
            d = x * 4 + zc
            t = d * chunks + c
            picked = jnp.concatenate([ctrl[idx_ref[k, t]] for k in range(neigh)], axis=1)
            out = jnp.dot(picked, loc[c, zc, x], preferred_element_type=jnp.float32)
            send[c, d] = out.astype(jnp.bfloat16)

    def part(c, values, src, acc):
        cols = pl.ds(c * TILE, TILE)
        weights = values[c, src].astype(jnp.float32).reshape(rows // 8, 1, 8, TILE)
        pert = ens[pl.ds(pl.multiple_of(src * per_dev, per_dev), per_dev), cols]
        pert = pert.astype(jnp.float32).reshape(rows // 8, 3, 8, TILE)
        return acc + jnp.sum(pert * weights, axis=0)

    def increment(c):
        acc = part(c, send, me, jnp.zeros((3, 8, TILE), jnp.float32))

        def step(i, acc):
            fwd_copy(c, i).wait_recv()
            return part(c, recv, source(i), acc)

        acc = lax.fori_loop(0, n_mem - 1, step, acc) * scale
        acc = jnp.concatenate([acc.reshape(24, TILE), jnp.zeros((PAD - 24, TILE), jnp.float32)], axis=0)
        incg[c, mine, :] = acc.astype(jnp.bfloat16)
        repeat(1, n_lev, lambda j: inc_copy(c, j).start())

    def observe(c):
        repeat(1, n_lev, lambda j: inc_copy(c, j).wait_recv())
        cols = pl.ds(c * TILE, TILE)
        evolved = lax.dot_general(
            opg[...], incg[c], (((0,), (0,)), ((), ())), preferred_element_type=jnp.float32
        )
        weighted = (prec_ref[:, cols] * evolved).astype(jnp.bfloat16)
        grad = jnp.dot(opg[mine, :], weighted, preferred_element_type=jnp.float32)
        grad = grad.astype(jnp.bfloat16).astype(jnp.float32)[:24].reshape(1, 3, 8, TILE)

        def back(d):
            pert = ens[pl.ds(pl.multiple_of(d * per_dev, per_dev), per_dev), cols]
            pert = pert.astype(jnp.float32).reshape(rows // 8, 3, 8, TILE)
            out = jnp.sum(pert * grad, axis=1) * scale
            bsend[c, d] = out.reshape(rows, TILE).astype(jnp.bfloat16)

        repeat(0, n_mem, back)

    half = n_mem // 2

    def send_fwd(c, lo=0, hi=n_mem - 1):
        repeat(lo, hi, lambda i: fwd_copy(c, i).start())

    def own_copy(c):
        return pltpu.make_async_copy(bsend.at[c, me], back_hbm.at[c, me], own_sem.at[c])

    def send_bwd(c, lo=0, hi=n_mem - 1):
        repeat(lo, hi, lambda i: bwd_copy(c, i).start())
        if lo == 0:
            own_copy(c).start()

    def first(n):
        loc_copy(n + groups + 1).start()
        localize(n)

    def send_group(n):
        c, g = lax.div(n, 4), lax.rem(n, 4)
        for u in range(4):
            if u < 3:
                fwd_copy(c, g * 4 + u).start()
            else:
                pl.when(g < 3)(lambda: fwd_copy(c, g * 4 + 3).start())

    def first_sent(n):
        first(n)
        send_group(n)

    def later_sent(n):
        localize(n)
        send_group(n)

    repeat(0, 4, first)
    pl.semaphore_wait(barrier, n_mem - 1 + n_lev - 1)
    send_fwd(0)
    repeat(1, n_lev, lambda j: op_copy(j).start())
    repeat(4, chunks * 4 - groups - 1, first_sent)
    ens_copy.start()
    prec_copy.start()
    later_sent(chunks * 4 - groups - 1)
    repeat(8, 10, later_sent)
    repeat(10, 16, localize)
    ens_copy.wait()
    prec_copy.wait()
    increment(0)
    send_fwd(2, half)
    send_fwd(3, 0, half)
    increment(1)
    send_fwd(3, half)
    repeat(1, n_lev, lambda j: op_copy(j).wait())
    observe(0)
    send_bwd(0, 0, half)
    increment(2)
    send_bwd(0, half)
    observe(1)
    send_bwd(1, 0, half)
    increment(3)
    send_bwd(1, half)
    observe(2)
    send_bwd(2)
    observe(3)
    send_bwd(3)

    for c in range(chunks):
        own_copy(c).wait()

        def finish(i):
            fwd_copy(c, i).wait_send()
            bwd_copy(c, i).wait()

        repeat(0, n_mem - 1, finish)
        repeat(1, n_lev, lambda j: inc_copy(c, j).wait_send())


def adjoint_kernel(chunks, neigh, idx_ref, ctrl_hbm, back_ref, loc_hbm, out_hbm, acc, loc, ctrl_sem, loc_sem, out_sem):
    tiles = loc.shape[0]
    groups = loc_sem.shape[0]
    per_group = tiles // groups

    def loc_copy(g):
        at = pl.ds(g * per_group, per_group)
        return pltpu.make_async_copy(loc_hbm.at[at], loc.at[at], loc_sem.at[g])

    ctrl_copy = pltpu.make_async_copy(ctrl_hbm, acc, ctrl_sem)
    ctrl_copy.start()
    for g in range(AHEAD):
        loc_copy(g).start()
    ctrl_copy.wait()

    def group(g, carry):
        @pl.when(g + AHEAD < groups)
        def _():
            loc_copy(g + AHEAD).start()

        loc_copy(g).wait()
        for u in range(per_group):
            t = g * per_group + u
            vals = lax.dot_general(
                back_ref[t % chunks, t // chunks], loc[t], (((1,), (1,)), ((), ())),
                preferred_element_type=jnp.float32,
            )
            for k in range(neigh):
                cols = pl.ds(pl.multiple_of(idx_ref[k, t] * TILE, TILE), TILE)
                acc[:, cols] += vals[:, k * TILE : (k + 1) * TILE]
        return carry

    lax.fori_loop(0, groups, group, 0)
    out = pltpu.make_async_copy(acc, out_hbm, out_sem)
    out.start()
    out.wait()


def body(n_mem, n_lev, control_vec, ens_perturb, loc_blocks, tile_index, obs_weight, channel_level_mask, obs_precision):
    mem_rows, lev_rows, points = control_vec.shape
    members = ens_perturb.shape[0]
    tiles, neigh = tile_index.shape
    chunks = tiles // n_mem
    rows = mem_rows * lev_rows
    channels = obs_weight.shape[2]
    control = control_vec.reshape(rows, points)
    index = tile_index.T
    ens = ens_perturb.reshape(members * 3 * lev_rows, points // n_mem)
    loc = loc_blocks.reshape(tiles, neigh * TILE, TILE)
    hbm = pl.BlockSpec(memory_space=pl.ANY)
    vmem = pl.BlockSpec(memory_space=pltpu.VMEM)
    smem = pl.BlockSpec(memory_space=pltpu.SMEM)
    dma = pltpu.SemaphoreType.DMA
    geo = (n_mem, n_lev, chunks, neigh, 1.0 / math.sqrt(members - 1))
    wide = (chunks, n_mem, rows, TILE)
    back = pl.pallas_call(
        functools.partial(exchange_kernel, geo),
        out_shape=jax.ShapeDtypeStruct(wide, jnp.bfloat16),
        in_specs=[smem, hbm, hbm, hbm, vmem, vmem, hbm],
        out_specs=hbm,
        scratch_shapes=[
            pltpu.VMEM(obs_precision.shape, jnp.float32),
            dma,
            pltpu.VMEM((rows, points), jnp.float32),
            pltpu.VMEM((tiles, rows, TILE), jnp.bfloat16),
            pltpu.VMEM((chunks, 4, 4, neigh * TILE, TILE), jnp.bfloat16),
            pltpu.VMEM(ens.shape, jnp.bfloat16),
            pltpu.VMEM(wide, jnp.bfloat16),
            pltpu.VMEM(wide, jnp.bfloat16),
            pltpu.VMEM(wide, jnp.bfloat16),
            pltpu.VMEM((n_lev * PAD, channels), jnp.bfloat16),
            pltpu.VMEM((chunks, n_lev * PAD, TILE), jnp.bfloat16),
            dma((8,)), dma((chunks * 4,)), dma, dma((chunks,)),
            dma((chunks, n_mem)), dma((chunks, n_mem)), dma((chunks, n_mem)), dma((chunks, n_mem)),
            dma((n_lev,)), dma((n_lev,)), dma((chunks, n_lev)), dma((chunks, n_lev)),
        ],
        compiler_params=pltpu.CompilerParams(
            collective_id=0, has_side_effects=True, vmem_limit_bytes=56 * 2**20
        ),
        name="exchange",
    )(index, control, ens, loc.reshape(4, 4, chunks, neigh * TILE, TILE), obs_weight, channel_level_mask, obs_precision)
    out = pl.pallas_call(
        functools.partial(adjoint_kernel, chunks, neigh),
        out_shape=jax.ShapeDtypeStruct((rows, points), jnp.float32),
        in_specs=[smem, hbm, vmem, hbm],
        out_specs=hbm,
        scratch_shapes=[
            pltpu.VMEM((rows, points), jnp.float32),
            pltpu.VMEM(loc.shape, jnp.bfloat16),
            dma, dma((16,)), dma,
        ],
        compiler_params=pltpu.CompilerParams(vmem_limit_bytes=48 * 2**20),
        name="adjoint",
    )(index, control, back, loc)
    return out.reshape(control_vec.shape)


def solution(mesh):
    return jax.shard_map(
        functools.partial(body, mesh.shape["mem"], mesh.shape["lev"]),
        mesh=mesh,
        in_specs=(
            P("mem", "lev", None),
            P(None, None, "lev", "mem"),
            P(),
            P(),
            P(None, "lev", None),
            P("lev", None),
            P(None, "mem"),
        ),
        out_specs=P("mem", "lev", None),
        check_vma=False,
    )
```

time: 101 us -> 86.5 us (0.86)
  Pallas kernels: 97.8 us -> 84.4 us
  local copies, waits for them, and re-layouts: 2.98 us -> 1.59 us
    pallas_call x1, Pallas kernels: 75.5 us -> 66.9 us  [body(): pl.pallas_call(functools.partial(exchange_kernel, geo), out_shape=jax.Sha...]
    pallas_call x1, Pallas kernels: 22.3 us -> 17.5 us  [body(): pl.pallas_call(functools.partial(adjoint_kernel, chunks, neigh), out_shap...]
    unnamed x5 -> x4, local copies, waits for them, and re-layouts: 2.98 us -> 1.59 us
where the time goes in v2:
time: 86.5 us; the launch traced here: 86 us
  Pallas kernels  84.4 us (98%)
  local copies, waits for them, and re-layouts  1.59 us (2%)
    pallas_call x1, Pallas kernels, body(): pl.pallas_call(functools.partial(exchange_kernel, geo), out_shape=jax.Sha...  66.9 us
    pallas_call x1, Pallas kernels, body(): pl.pallas_call(functools.partial(adjoint_kernel, chunks, neigh), out_shap...  17.5 us

profile of v2, /device:TPU:0, one launch (start us, length us, event | category | flops | bytes accessed | tf_op | source)
XLA Modules:
  0.0 86.0 jit_solution(6097144063156259535)
XLA Ops:
  0.0 0.0 copy-start.1
  0.0 66.9 %exchange.1.back_ref = bf16[4,16,128,128]{3,2,1,0:T(8,128)(2,1)} custom-call(s32[9,64]{1,0:T(8,128)} %bitcast.6, f32[128,8192]{1,0:T(8,128)} %bitcast.10, bf16[6144,512]{1,0:T(8,128)(2,1)} %bitcast.12, bf16[4,4,4,1152,128]{4,3,2,1,0:T(8,128)(2,1)} %bitcast.8, bf16[3,8,256]{2,1,0:T(8,128)(2,1)} %obs_ref.1, s32[8,256]{1,0:T(8,128)} %mask_ref.1, ...), custom_call_target="tpu_custom_call" | custom-call | tf_op jit(solution)/shard_map/exchange/pallas_call | solution.py:291
  66.9 0.0 copy-done.1
  66.9 0.0 copy-start
  66.9 1.6 %copy-done = bf16[4,16,128,128]{3,2,1,0:T(8,128)(2,1)S(1)} copy-done((bf16[4,16,128,128]{3,2,1,0:T(8,128)(2,1)S(1)}, bf16[4,16,128,128]{3,2,1,0:T(8,128)(2,1)}, u32[]{:S(2)}) %copy-start) | copy-done | bytes 2097176
  68.5 17.5 %adjoint.1 = f32[128,8192]{1,0:T(8,128)} custom-call(s32[9,64]{1,0:T(8,128)S(1)} %bitcast.7, f32[128,8192]{1,0:T(8,128)} %bitcast.11, bf16[4,16,128,128]{3,2,1,0:T(8,128)(2,1)S(1)} %copy-done, bf16[64,1152,128]{2,1,0:T(8,128)(2,1)} %bitcast.9), custom_call_target="tpu_custom_call" | custom-call | tf_op jit(solution)/shard_map/adjoint/pallas_call | solution.py:317
Async XLA Ops:
  0.0 66.9 %copy-start.1 = (s32[64,9]{0,1:T(8,128)S(1)}, s32[64,9]{0,1:T(8,128)}, u32[]{:S(2)}) copy-start(s32[64,9]{0,1:T(8,128)} %param.10) | copy-start | bytes 6916
  66.9 1.6 %copy-start = (bf16[4,16,128,128]{3,2,1,0:T(8,128)(2,1)S(1)}, bf16[4,16,128,128]{3,2,1,0:T(8,128)(2,1)}, u32[]{:S(2)}) copy-start(bf16[4,16,128,128]{3,2,1,0:T(8,128)(2,1)} %exchange.1.back_ref) | copy-start | bytes 6291460

commit v3 on v2

--- a/solution.py
+++ b/solution.py
@@ -11,15 +11,19 @@
 MESH = pl.DeviceIdType.MESH
 TILE = 128
 PAD = 32
-AHEAD = 3
+KEEP = 3
+SLOTS = 104
+WAYS = 16
+UNROLL = 13
 
 
 def exchange_kernel(
-    geo, idx_ref, ctrl_hbm, ens_hbm, loc_hbm, obs_ref, mask_ref, prec_hbm, back_hbm,
-    prec_ref, prec_sem, ctrl32, ctrl, loc, ens, send, recv, bsend, opg, incg,
+    geo, idx_ref, idx_vec, ctrl_hbm, ens_hbm, loc_hbm, obs_ref, mask_ref, prec_hbm, back_hbm, part_hbm,
+    arrived0, arrived1, arrived2, sums, table_vec, table, table_sem, part_sem, prec_ref, prec_sem, ctrl32, ctrl, loc, ens, send, recv, bsend, opg, incg,
     ctrl_sem, loc_sem, ens_sem, own_sem, fsend, frecv, bsend_sem, brecv_sem, osend, orecv, isend, irecv,
 ):
     n_mem, n_lev, chunks, neigh, scale = geo
+    arrived = (arrived0, arrived1, arrived2)
     me = lax.axis_index("mem")
     lev = lax.axis_index("lev")
     my_x, my_z, my_c = lax.div(me, 4), lax.rem(lax.div(me, 2), 2), lax.rem(me, 2)
@@ -83,6 +87,59 @@
 
     repeat(0, groups, convert)
 
+    def tabulate(c):
+        target = lax.broadcasted_iota(jnp.int32, (64, 64), 0)
+        idx = idx_vec[...]
+        hits = jnp.zeros((64, 64), jnp.int32)
+        for k in range(neigh):
+            hits = hits + jnp.where(target == idx[k : k + 1, :], k + 1, 0)
+        hits = jnp.minimum(hits, neigh)
+        lane = lax.broadcasted_iota(jnp.int32, (64, TILE), 1)
+
+        def column(d):
+            at = d * chunks + c
+            return jnp.broadcast_to(hits[:, at : at + 1], (64, TILE))
+
+        count = jnp.zeros((64, TILE), jnp.int32)
+        for d in range(n_mem):
+            count = count + jnp.minimum(column(d), 1)
+        pairs = lax.div(count + 1, 2)
+        slot = lane[:1]
+        end = jnp.zeros((1, TILE), jnp.int32)
+        base = jnp.zeros((1, TILE), jnp.int32)
+        for s in range(64):
+            table_vec[c, 8 + s : 9 + s] = end
+            end = end + pairs[s : s + 1]
+            base = jnp.where(end <= slot, end, base)
+        begin = table_vec[c, 8:]
+        even = jnp.zeros((64, TILE), jnp.int32)
+        odd = jnp.zeros((64, TILE), jnp.int32)
+        seen = jnp.zeros((64, TILE), jnp.int32)
+        for d in range(n_mem):
+            value = column(d)
+            here = jnp.where((lane == begin + lax.div(seen, 2)) & (value > 0), value + d * WAYS, 0)
+            second = lax.rem(seen, 2)
+            even = even + here * (1 - second)
+            odd = odd + here * second
+            seen = seen + jnp.minimum(value, 1)
+
+        def codes(values):
+            for size in (32, 16, 8):
+                values = values[:size] + values[size:]
+            total = values[0:1]
+            for s in range(1, 8):
+                total = total + values[s : s + 1]
+            return jnp.where(total > 0, total - 1, WAYS * n_mem)
+
+        row = lax.broadcasted_iota(jnp.int32, (8, TILE), 0)
+        head = jnp.where(row == 0, codes(even), jnp.where(row == 1, codes(odd), slot - base))
+        table_vec[c, :8] = head
+        last = jnp.maximum(begin + pairs - 1, 0)
+        table_vec[c, 8:] = jnp.where(lane == 1, jnp.minimum(count, 1), last)
+        arrived[c][n_mem] = jnp.zeros((rows, TILE), jnp.bfloat16)
+
+    table_copy = pltpu.make_async_copy(table_vec, table, table_sem)
+
     def op_copy(j):
         return pltpu.make_async_remote_copy(
             src_ref=opg.at[mine], dst_ref=opg.at[mine], send_sem=osend.at[j], recv_sem=orecv.at[j],
@@ -103,10 +160,13 @@
             device_id={"mem": d}, device_id_type=MESH,
         )
 
+    def landing(c):
+        return arrived[c].at[me] if c < KEEP else back_hbm.at[c - KEEP, me]
+
     def bwd_copy(c, i):
         d = peer(i)
         return pltpu.make_async_remote_copy(
-            src_ref=bsend.at[c, d], dst_ref=back_hbm.at[c, me], send_sem=bsend_sem.at[c, i],
+            src_ref=bsend.at[c, d], dst_ref=landing(c), send_sem=bsend_sem.at[c, i],
             recv_sem=brecv_sem.at[c, i], device_id={"mem": d}, device_id_type=MESH,
         )
 
@@ -118,7 +178,7 @@
             d = x * 4 + zc
             t = d * chunks + c
             picked = jnp.concatenate([ctrl[idx_ref[k, t]] for k in range(neigh)], axis=1)
-            out = jnp.dot(picked, loc[c, zc, x], preferred_element_type=jnp.float32)
+            out = jnp.dot(picked, loc[c, zc, x].reshape(neigh * TILE, TILE), preferred_element_type=jnp.float32)
             send[c, d] = out.astype(jnp.bfloat16)
 
     def part(c, values, src, acc):
@@ -164,7 +224,7 @@
         repeat(lo, hi, lambda i: fwd_copy(c, i).start())
 
     def own_copy(c):
-        return pltpu.make_async_copy(bsend.at[c, me], back_hbm.at[c, me], own_sem.at[c])
+        return pltpu.make_async_copy(bsend.at[c, me], landing(c), own_sem.at[c])
 
     def send_bwd(c, lo=0, hi=n_mem - 1):
         repeat(lo, hi, lambda i: bwd_copy(c, i).start())
@@ -190,6 +250,44 @@
     def later_sent(n):
         localize(n)
         send_group(n)
+
+    def part_copy(g):
+        cols = pl.ds(pl.multiple_of(g * span, TILE), span)
+        return pltpu.make_async_copy(ctrl32.at[:, cols], part_hbm.at[:, cols], part_sem.at[g])
+
+    def gather(c):
+        own_copy(c).wait()
+        repeat(0, n_mem - 1, lambda i: bwd_copy(c, i).wait_recv())
+
+        def block(code):
+            d, k = lax.div(code, WAYS), lax.rem(code, WAYS)
+            x, zc = lax.rem(lax.div(d, 4), 4), lax.rem(d, 4)
+            return arrived[c][d], loc[c, zc, x, k]
+
+        def slots(q, before):
+            for u in range(UNROLL):
+                p = q * UNROLL + u
+                left, right = zip(block(table[c, 0, p]), block(table[c, 1, p]))
+                value = lax.dot_general(
+                    jnp.concatenate(left, axis=1), jnp.concatenate(right, axis=1), (((1,), (1,)), ((), ())),
+                    preferred_element_type=jnp.float32,
+                )
+                before = value + jnp.minimum(table[c, 2, p], 1).astype(jnp.float32) * before
+                sums[p] = before
+            return before
+
+        lax.fori_loop(0, SLOTS // UNROLL, slots, jnp.zeros((rows, TILE), jnp.float32))
+
+        def settle(g):
+            for u in range(per_group):
+                s = g * per_group + u
+                cols = pl.ds(pl.multiple_of(s * TILE, TILE), TILE)
+                present = table[c, 8 + s, 1].astype(jnp.float32)
+                ctrl32[:, cols] += present * sums[table[c, 8 + s, 0]]
+            if c == KEEP - 1:
+                part_copy(g).start()
+
+        repeat(0, groups, settle)
 
     repeat(0, 4, first)
     pl.semaphore_wait(barrier, n_mem - 1 + n_lev - 1)
@@ -209,63 +307,76 @@
     increment(1)
     send_fwd(3, half)
     repeat(1, n_lev, lambda j: op_copy(j).wait())
+    tabulate(0)
+    tabulate(1)
     observe(0)
     send_bwd(0, 0, half)
     increment(2)
     send_bwd(0, half)
     observe(1)
     send_bwd(1, 0, half)
+    tabulate(2)
+    table_copy.start()
     increment(3)
     send_bwd(1, half)
     observe(2)
     send_bwd(2)
+    table_copy.wait()
+    gather(0)
     observe(3)
     send_bwd(3)
+    for c in range(1, KEEP):
+        gather(c)
 
     for c in range(chunks):
-        own_copy(c).wait()
+        if c >= KEEP:
+            own_copy(c).wait()
 
         def finish(i):
             fwd_copy(c, i).wait_send()
-            bwd_copy(c, i).wait()
+            bwd_copy(c, i).wait_send()
+            if c >= KEEP:
+                bwd_copy(c, i).wait_recv()
 
         repeat(0, n_mem - 1, finish)
         repeat(1, n_lev, lambda j: inc_copy(c, j).wait_send())
-
-
-def adjoint_kernel(chunks, neigh, idx_ref, ctrl_hbm, back_ref, loc_hbm, out_hbm, acc, loc, ctrl_sem, loc_sem, out_sem):
-    tiles = loc.shape[0]
-    groups = loc_sem.shape[0]
-    per_group = tiles // groups
-
-    def loc_copy(g):
-        at = pl.ds(g * per_group, per_group)
-        return pltpu.make_async_copy(loc_hbm.at[at], loc.at[at], loc_sem.at[g])
-
-    ctrl_copy = pltpu.make_async_copy(ctrl_hbm, acc, ctrl_sem)
-    ctrl_copy.start()
-    for g in range(AHEAD):
-        loc_copy(g).start()
-    ctrl_copy.wait()
+    repeat(0, groups, lambda g: part_copy(g).wait())
+
+
+def adjoint_kernel(
+    chunks, neigh, idx_ref, part_hbm, back_hbm, loc_hbm, out_hbm, acc, back, loc, part_sem, back_sem, loc_sem, out_sem
+):
+    steps = loc_sem.shape[0]
+    n_mem = back.shape[1]
+
+    def loc_copy(n):
+        return pltpu.make_async_copy(loc_hbm.at[n % n_mem, KEEP + n // n_mem], loc.at[n], loc_sem.at[n])
+
+    back_copy = pltpu.make_async_copy(back_hbm, back, back_sem)
+    part_copy = pltpu.make_async_copy(part_hbm, acc, part_sem)
+    part_copy.start()
+    back_copy.start()
+    for n in range(steps):
+        loc_copy(n).start()
+    back_copy.wait()
+    part_copy.wait()
 
     def group(g, carry):
-        @pl.when(g + AHEAD < groups)
-        def _():
-            loc_copy(g + AHEAD).start()
-
-        loc_copy(g).wait()
-        for u in range(per_group):
-            t = g * per_group + u
+        for u in range(4):
+            loc_copy(g * 4 + u).wait()
+        for u in range(4):
+            n = g * 4 + u
+            c, d = n // n_mem, n % n_mem
+            t = d * chunks + c + KEEP
             vals = lax.dot_general(
-                back_ref[t % chunks, t // chunks], loc[t], (((1,), (1,)), ((), ())),
-                preferred_element_type=jnp.float32,
+                back[c, d], loc[n], (((1,), (1,)), ((), ())), preferred_element_type=jnp.float32
             )
             for k in range(neigh):
                 cols = pl.ds(pl.multiple_of(idx_ref[k, t] * TILE, TILE), TILE)
                 acc[:, cols] += vals[:, k * TILE : (k + 1) * TILE]
         return carry
 
-    lax.fori_loop(0, groups, group, 0)
+    lax.fori_loop(0, steps // 4, group, 0)
     out = pltpu.make_async_copy(acc, out_hbm, out_sem)
     out.start()
     out.wait()
@@ -282,23 +393,32 @@
     index = tile_index.T
     ens = ens_perturb.reshape(members * 3 * lev_rows, points // n_mem)
     loc = loc_blocks.reshape(tiles, neigh * TILE, TILE)
-    hbm = pl.BlockSpec(memory_space=pl.ANY)
+    hbm = pl.BlockSpec(memory_space=pltpu.HBM)
     vmem = pl.BlockSpec(memory_space=pltpu.VMEM)
     smem = pl.BlockSpec(memory_space=pltpu.SMEM)
     dma = pltpu.SemaphoreType.DMA
     geo = (n_mem, n_lev, chunks, neigh, 1.0 / math.sqrt(members - 1))
     wide = (chunks, n_mem, rows, TILE)
-    back = pl.pallas_call(
+    back, part = pl.pallas_call(
         functools.partial(exchange_kernel, geo),
-        out_shape=jax.ShapeDtypeStruct(wide, jnp.bfloat16),
-        in_specs=[smem, hbm, hbm, hbm, vmem, vmem, hbm],
-        out_specs=hbm,
+        out_shape=(
+            jax.ShapeDtypeStruct((chunks - KEEP,) + wide[1:], jnp.bfloat16),
+            jax.ShapeDtypeStruct((rows, points), jnp.float32),
+        ),
+        in_specs=[smem, vmem, hbm, hbm, hbm, vmem, vmem, hbm],
+        out_specs=(hbm, hbm),
         scratch_shapes=[
+            *[pltpu.VMEM((n_mem + 1, rows, TILE), jnp.bfloat16)] * KEEP,
+            pltpu.VMEM((SLOTS, rows, TILE), jnp.float32),
+            pltpu.VMEM((KEEP, 72, TILE), jnp.int32),
+            pltpu.SMEM((KEEP, 72, TILE), jnp.int32),
+            dma,
+            dma((8,)),
             pltpu.VMEM(obs_precision.shape, jnp.float32),
             dma,
             pltpu.VMEM((rows, points), jnp.float32),
             pltpu.VMEM((tiles, rows, TILE), jnp.bfloat16),
-            pltpu.VMEM((chunks, 4, 4, neigh * TILE, TILE), jnp.bfloat16),
+            pltpu.VMEM((chunks, 4, 4, neigh, TILE, TILE), jnp.bfloat16),
             pltpu.VMEM(ens.shape, jnp.bfloat16),
             pltpu.VMEM(wide, jnp.bfloat16),
             pltpu.VMEM(wide, jnp.bfloat16),
@@ -313,20 +433,22 @@
             collective_id=0, has_side_effects=True, vmem_limit_bytes=56 * 2**20
         ),
         name="exchange",
-    )(index, control, ens, loc.reshape(4, 4, chunks, neigh * TILE, TILE), obs_weight, channel_level_mask, obs_precision)
+    )(index, index, control, ens, loc_blocks.reshape(4, 4, chunks, neigh, TILE, TILE), obs_weight, channel_level_mask, obs_precision)
+    late = (chunks - KEEP) * n_mem
     out = pl.pallas_call(
         functools.partial(adjoint_kernel, chunks, neigh),
         out_shape=jax.ShapeDtypeStruct((rows, points), jnp.float32),
-        in_specs=[smem, hbm, vmem, hbm],
+        in_specs=[smem, hbm, hbm, hbm],
         out_specs=hbm,
         scratch_shapes=[
             pltpu.VMEM((rows, points), jnp.float32),
-            pltpu.VMEM(loc.shape, jnp.bfloat16),
-            dma, dma((16,)), dma,
+            pltpu.VMEM(back.shape, jnp.bfloat16),
+            pltpu.VMEM((late, neigh * TILE, TILE), jnp.bfloat16),
+            dma, dma, dma((late,)), dma,
         ],
-        compiler_params=pltpu.CompilerParams(vmem_limit_bytes=48 * 2**20),
+        compiler_params=pltpu.CompilerParams(vmem_limit_bytes=63 * 2**20),
         name="adjoint",
-    )(index, control, back, loc)
+    )(index, part, back, loc.reshape(n_mem, chunks, neigh * TILE, TILE))
     return out.reshape(control_vec.shape)
 
 

time: 86.5 us -> 80.5 us (0.931)
  Pallas kernels: 84.4 us -> 80.3 us
  local copies, waits for them, and re-layouts: 1.59 us -> 0 us
    pallas_call x1, Pallas kernels: 17.5 us -> 9.6 us  [body(): pl.pallas_call(functools.partial(adjoint_kernel, chunks, neigh), out_shap...]
    pallas_call x1, Pallas kernels: 66.9 us -> 70.7 us  [body(): pl.pallas_call(functools.partial(exchange_kernel, geo), out_shape=(jax.Sh...]
    unnamed x4 -> x0, local copies, waits for them, and re-layouts: 1.59 us -> none
where the time goes in v3:
time: 80.5 us; the launch traced here: 80.3 us
  Pallas kernels  80.3 us (100%)
    pallas_call x1, Pallas kernels, body(): pl.pallas_call(functools.partial(exchange_kernel, geo), out_shape=(jax.Sh...  70.7 us
    pallas_call x1, Pallas kernels, body(): pl.pallas_call(functools.partial(adjoint_kernel, chunks, neigh), out_shap...  9.6 us

profile of v3, /device:TPU:0, one launch (start us, length us, event | category | flops | bytes accessed | tf_op | source)
XLA Modules:
  0.0 80.3 jit_solution(9906635380614419909)
XLA Ops:
  0.0 70.7 %exchange.1 = (bf16[1,16,128,128]{3,2,1,0:T(8,128)(2,1)}, f32[128,8192]{1,0:T(8,128)}) custom-call(s32[9,64]{1,0:T(8,128)} %bitcast.10, s32[9,64]{1,0:T(8,128)} %bitcast.11, f32[128,8192]{1,0:T(8,128)} %bitcast.9, bf16[6144,512]{1,0:T(8,128)(2,1)} %bitcast.8, bf16[4,4,4,9,128,128]{5,4,3,2,1,0:T(8,128)(2,1)} %bitcast.6, bf16[3,8,256]{2,1,0:T(8,128)(2,1)} %obs_ref.1, ...), custom_call_target="tpu_custom_call" | custom-call | tf_op jit(solution)/shard_map/exchange/pallas_call | solution.py:402
  70.7 9.6 %adjoint.1 = f32[128,8192]{1,0:T(8,128)} custom-call(s32[9,64]{1,0:T(8,128)} %bitcast.12, f32[128,8192]{1,0:T(8,128)} %get-tuple-element.7.part_hbm, bf16[1,16,128,128]{3,2,1,0:T(8,128)(2,1)} %get-tuple-element.8.back_hbm, bf16[16,4,1152,128]{3,2,1,0:T(8,128)(2,1)} %bitcast.7), custom_call_target="tpu_custom_call" | custom-call | tf_op jit(solution)/shard_map/adjoint/pallas_call | solution.py:438

commit v4 on v3

--- a/solution.py
+++ b/solution.py
@@ -289,9 +289,10 @@
 
         repeat(0, groups, settle)
 
-    repeat(0, 4, first)
+    first(0)
     pl.semaphore_wait(barrier, n_mem - 1 + n_lev - 1)
-    send_fwd(0)
+    send_group(0)
+    repeat(1, 4, first_sent)
     repeat(1, n_lev, lambda j: op_copy(j).start())
     repeat(4, chunks * 4 - groups - 1, first_sent)
     ens_copy.start()
@@ -344,7 +345,7 @@
 
 
 def adjoint_kernel(
-    chunks, neigh, idx_ref, part_hbm, back_hbm, loc_hbm, out_hbm, acc, back, loc, part_sem, back_sem, loc_sem, out_sem
+    chunks, neigh, idx_ref, part_hbm, back_hbm, loc_hbm, out_hbm, acc, part, back, loc, part_sem, back_sem, loc_sem, out_sem
 ):
     steps = loc_sem.shape[0]
     n_mem = back.shape[1]
@@ -353,13 +354,13 @@
         return pltpu.make_async_copy(loc_hbm.at[n % n_mem, KEEP + n // n_mem], loc.at[n], loc_sem.at[n])
 
     back_copy = pltpu.make_async_copy(back_hbm, back, back_sem)
-    part_copy = pltpu.make_async_copy(part_hbm, acc, part_sem)
-    part_copy.start()
+    part_copy = pltpu.make_async_copy(part_hbm, part, part_sem)
     back_copy.start()
     for n in range(steps):
         loc_copy(n).start()
+    part_copy.start()
+    acc[...] = jnp.zeros_like(acc)
     back_copy.wait()
-    part_copy.wait()
 
     def group(g, carry):
         for u in range(4):
@@ -377,9 +378,26 @@
         return carry
 
     lax.fori_loop(0, steps // 4, group, 0)
-    out = pltpu.make_async_copy(acc, out_hbm, out_sem)
-    out.start()
-    out.wait()
+    part_copy.wait()
+    pieces = out_sem.shape[0]
+    span = acc.shape[1] // pieces
+
+    def out_copy(g):
+        cols = pl.ds(pl.multiple_of(g * span, TILE), span)
+        return pltpu.make_async_copy(acc.at[:, cols], out_hbm.at[:, cols], out_sem.at[g])
+
+    def close(g, carry):
+        cols = pl.ds(pl.multiple_of(g * span, TILE), span)
+        acc[:, cols] += part[:, cols]
+        out_copy(g).start()
+        return carry
+
+    def drain(g, carry):
+        out_copy(g).wait()
+        return carry
+
+    lax.fori_loop(0, pieces, close, 0)
+    lax.fori_loop(0, pieces, drain, 0)
 
 
 def body(n_mem, n_lev, control_vec, ens_perturb, loc_blocks, tile_index, obs_weight, channel_level_mask, obs_precision):
@@ -442,9 +460,10 @@
         out_specs=hbm,
         scratch_shapes=[
             pltpu.VMEM((rows, points), jnp.float32),
+            pltpu.VMEM((rows, points), jnp.float32),
             pltpu.VMEM(back.shape, jnp.bfloat16),
             pltpu.VMEM((late, neigh * TILE, TILE), jnp.bfloat16),
-            dma, dma, dma((late,)), dma,
+            dma, dma, dma((late,)), dma((8,)),
         ],
         compiler_params=pltpu.CompilerParams(vmem_limit_bytes=63 * 2**20),
         name="adjoint",

time: 80.5 us -> 78.8 us (0.979)
  Pallas kernels: 80.3 us -> 78.5 us
    pallas_call x1, Pallas kernels: 9.6 us -> 8.49 us  [body(): pl.pallas_call(functools.partial(adjoint_kernel, chunks, neigh), out_shap...]
where the time goes in v4:
time: 78.8 us; the launch traced here: 78.6 us
  Pallas kernels  78.5 us (100%)
    pallas_call x1, Pallas kernels, body(): pl.pallas_call(functools.partial(exchange_kernel, geo), out_shape=(jax.Sh...  70.1 us
    pallas_call x1, Pallas kernels, body(): pl.pallas_call(functools.partial(adjoint_kernel, chunks, neigh), out_shap...  8.49 us

profile of v4, /device:TPU:0, one launch (start us, length us, event | category | flops | bytes accessed | tf_op | source)
XLA Modules:
  0.0 78.6 jit_solution(8029020757007312367)
XLA Ops:
  0.0 70.1 %exchange.1 = (bf16[1,16,128,128]{3,2,1,0:T(8,128)(2,1)}, f32[128,8192]{1,0:T(8,128)}) custom-call(s32[9,64]{1,0:T(8,128)} %bitcast.10, s32[9,64]{1,0:T(8,128)} %bitcast.11, f32[128,8192]{1,0:T(8,128)} %bitcast.9, bf16[6144,512]{1,0:T(8,128)(2,1)} %bitcast.8, bf16[4,4,4,9,128,128]{5,4,3,2,1,0:T(8,128)(2,1)} %bitcast.6, bf16[3,8,256]{2,1,0:T(8,128)(2,1)} %obs_ref.1, ...), custom_call_target="tpu_custom_call" | custom-call | tf_op jit(solution)/shard_map/exchange/pallas_call | solution.py:420
  70.1 8.5 %adjoint.1 = f32[128,8192]{1,0:T(8,128)} custom-call(s32[9,64]{1,0:T(8,128)} %bitcast.12, f32[128,8192]{1,0:T(8,128)} %get-tuple-element.7.part_hbm, bf16[1,16,128,128]{3,2,1,0:T(8,128)(2,1)} %get-tuple-element.8.back_hbm, bf16[16,4,1152,128]{3,2,1,0:T(8,128)(2,1)} %bitcast.7), custom_call_target="tpu_custom_call" | custom-call | tf_op jit(solution)/shard_map/adjoint/pallas_call | solution.py:456

commit v5 on v4

--- a/solution.py
+++ b/solution.py
@@ -356,15 +356,24 @@
     back_copy = pltpu.make_async_copy(back_hbm, back, back_sem)
     part_copy = pltpu.make_async_copy(part_hbm, part, part_sem)
     back_copy.start()
-    for n in range(steps):
+    for n in range(8):
         loc_copy(n).start()
-    part_copy.start()
     acc[...] = jnp.zeros_like(acc)
     back_copy.wait()
 
     def group(g, carry):
         for u in range(4):
             loc_copy(g * 4 + u).wait()
+
+        @pl.when(g + 2 < steps // 4)
+        def _():
+            for u in range(4):
+                loc_copy(g * 4 + 8 + u).start()
+
+        @pl.when(g == 1)
+        def _():
+            part_copy.start()
+
         for u in range(4):
             n = g * 4 + u
             c, d = n // n_mem, n % n_mem

time: 78.8 us -> 78.7 us (level)
  no operation moved by 1% of the time
where the time goes in v5:
time: 78.7 us; the launch traced here: 78.4 us
  Pallas kernels  78.4 us (100%)
    pallas_call x1, Pallas kernels, body(): pl.pallas_call(functools.partial(exchange_kernel, geo), out_shape=(jax.Sh...  70.1 us
    pallas_call x1, Pallas kernels, body(): pl.pallas_call(functools.partial(adjoint_kernel, chunks, neigh), out_shap...  8.36 us

profile of v5, /device:TPU:0, one launch (start us, length us, event | category | flops | bytes accessed | tf_op | source)
XLA Modules:
  0.0 78.4 jit_solution(16610387909964898777)
XLA Ops:
  0.0 70.1 %exchange.1 = (bf16[1,16,128,128]{3,2,1,0:T(8,128)(2,1)}, f32[128,8192]{1,0:T(8,128)}) custom-call(s32[9,64]{1,0:T(8,128)} %bitcast.10, s32[9,64]{1,0:T(8,128)} %bitcast.11, f32[128,8192]{1,0:T(8,128)} %bitcast.9, bf16[6144,512]{1,0:T(8,128)(2,1)} %bitcast.8, bf16[4,4,4,9,128,128]{5,4,3,2,1,0:T(8,128)(2,1)} %bitcast.6, bf16[3,8,256]{2,1,0:T(8,128)(2,1)} %obs_ref.1, ...), custom_call_target="tpu_custom_call" | custom-call | tf_op jit(solution)/shard_map/exchange/pallas_call | solution.py:429
  70.1 8.4 %adjoint.1 = f32[128,8192]{1,0:T(8,128)} custom-call(s32[9,64]{1,0:T(8,128)} %bitcast.12, f32[128,8192]{1,0:T(8,128)} %get-tuple-element.7.part_hbm, bf16[1,16,128,128]{3,2,1,0:T(8,128)(2,1)} %get-tuple-element.8.back_hbm, bf16[16,4,1152,128]{3,2,1,0:T(8,128)(2,1)} %bitcast.7), custom_call_target="tpu_custom_call" | custom-call | tf_op jit(solution)/shard_map/adjoint/pallas_call | solution.py:465
